TPU v7x, 32 devices: a whole 2x2x4 slice. The times are simulated.
32 devices in a mesh: groups: 2 (over y), vocab: 8 (over z, x), mp: 2 (over core).
Axes of the slice: x: 2, y: 2, z: 4, core: 2. Of those that a mesh axis runs over, the one named last changes fastest.
Arguments:
- gate_pre: bfloat16 [32, 14336], P(('groups', 'vocab'), 'mp'), parts along dimension 0, may hold values from -6 to 6
- up_pre: bfloat16 [32, 14336], P(('groups', 'vocab'), 'mp'), parts along dimension 0, may hold values from -6 to 6
- down_weight: bfloat16 [8192, 14336], P('vocab', 'mp'), may hold values from -0.046875 to 0.046875
- residual: bfloat16 [32, 8192], P(('groups', 'vocab', 'mp')), parts along dimension 0, may hold values from -36 to 36
- norm_gain: bfloat16 [8192], replicated, may hold values from 0.5 to 1.5
- head_weight: bfloat16 [8192, 4032], P('mp', 'vocab')
- targets: int32 [32], P(('groups', 'mp')), parts along dimension 0, may hold values from 0 to 4031
Outputs:
- log_likelihood: float32 [32], P(('groups', 'mp')), parts along dimension 0
There are 2 independent parts, one for each index of `groups`. A program takes and returns all parts, laid end to end along the dimension named above; an argument that names none is the same for every part. Nothing has to cross between parts.
All inputs are finite; a program needn't handle non-finite values.
Results may differ from a plain program's by a relative error of at most 0.0003.
The roundings to bfloat16 on the way count: a program that leaves them out, or rounds other values in their place, can miss the bound.
Values may be sent and summed in bfloat16 or wider, within the bound.
A program may use at most 64 MiB of HBM per device.

v0:
```python
import jax
import jax.numpy as jnp
from jax import lax
from jax.sharding import PartitionSpec as P

EPSILON = 1e-05


def merged_2(value, axis, combine):
    everything = jax.tree.map(lambda part: lax.all_gather(part, axis), value)
    first = jax.tree.map(lambda part: part[0], everything)

    def turn(k, so_far):
        return combine(so_far, jax.tree.map(lambda part: part[k], everything))

    return lax.fori_loop(1, lax.axis_size(axis), turn, first)


def merge_stats(earlier, follows):
    joint_max = jnp.maximum(earlier[0], follows[0])
    joint_sum = earlier[1] * jnp.exp(earlier[0] - joint_max) + follows[1] * jnp.exp(
        follows[0] - joint_max
    )
    return (joint_max, joint_sum, earlier[2] + follows[2])


def body(gate_pre, up_pre, down_weight, residual, norm_gain, head_weight, targets):
    vocab_count = lax.axis_size("vocab")
    model_count = lax.axis_size("mp")
    model_index = lax.axis_index("mp")
    vocab_index = lax.axis_index("vocab")
    gated_units = (jax.nn.silu(gate_pre.astype(jnp.float32)) * up_pre.astype(jnp.float32)).astype(
        jnp.bfloat16
    )
    down_terms = lax.dot_general(
        lax.all_gather(gated_units, "vocab", axis=0, tiled=True),
        down_weight,
        (((1,), (1,)), ((), ())),
        preferred_element_type=jnp.float32,
    )
    own_rows = residual.shape[0]
    block_cols = down_weight.shape[0]
    grouped = down_terms.reshape(vocab_count, model_count, own_rows, block_cols)
    arrived = lax.all_to_all(
        lax.all_to_all(grouped, "vocab", split_axis=0, concat_axis=3, tiled=True),
        "mp",
        split_axis=1,
        concat_axis=0,
        tiled=True,
    )
    update = jnp.sum(arrived, axis=(0, 1))
    stream = (residual.astype(jnp.float32) + update).astype(jnp.bfloat16)
    stream = lax.optimization_barrier(stream)
    widened = stream.astype(jnp.float32)
    mean_square = jnp.mean(widened * widened, axis=1, keepdims=True)
    normed = (
        widened * lax.rsqrt(mean_square + EPSILON) * norm_gain.astype(jnp.float32)[None, :]
    ).astype(jnp.bfloat16)
    half_width = head_weight.shape[0]
    halves = lax.dynamic_slice_in_dim(
        lax.all_gather(normed, ("vocab", "mp"), axis=0, tiled=True),
        model_index * half_width,
        half_width,
        1,
    )
    logit_terms = jnp.dot(halves, head_weight, preferred_element_type=jnp.float32)
    logits = lax.psum_scatter(logit_terms, "mp", scatter_dimension=0, tiled=True)
    local_ids = targets - vocab_index * logits.shape[1]
    columns = lax.broadcasted_iota(jnp.int32, logits.shape, 1)
    chosen = jnp.sum(jnp.where(columns == local_ids[:, None], logits, 0.0), axis=1)
    row_top = jnp.max(logits, axis=1)
    exp_total = jnp.sum(jnp.exp(logits - row_top[:, None]), axis=1)
    merged = merged_2((row_top, exp_total, chosen), "vocab", merge_stats)
    return merged[2] - merged[0] - jnp.log(merged[1])


def solution(mesh):
    return jax.shard_map(
        body,
        mesh=mesh,
        in_specs=(
            P(("groups", "vocab"), "mp"),
            P(("groups", "vocab"), "mp"),
            P("vocab", "mp"),
            P(("groups", "vocab", "mp"), None),
            P(),
            P("mp", "vocab"),
            P(("groups", "mp")),
        ),
        out_specs=P(("groups", "mp")),
        check_vma=False,
    )
```

profile of v0, /device:TPU:0, one launch (start us, length us, event | category | flops | bytes accessed | tf_op | source)
XLA Modules:
  0.0 128.7 jit_solution(11626139243467973319)
XLA Ops:
  6.5 0.9 fusion.12
  7.4 32.5 %all-gather.3 = bf16[8,2,7168]{2,1,0:T(2,128)(2,1)S(1)} all-gather(bf16[1,2,7168]{2,1,0:T(2,128)(2,1)S(1)} %fusion.12), channel_id=1, replica_groups=mesh['groups'=2,'vocab'=8,'mp'=2] {'vocab'}, dimensions={0}, use_global_device_ids=true | all-gather | bytes 258048 | tf_op jit(solution)/shard_map/all_gather | solution.py:36
  39.9 0.1 reshape.39
  40.0 9.1 %fusion.14 = f32[16,1024]{1,0:T(8,128)S(1)} fusion(bf16[16,7168]{1,0:T(8,128)(2,1)S(1)} %reshape.39, bf16[1024,7168]{1,0:T(8,128)(2,1)} %param.11), kind=kOutput, calls=%fused_computation.28 | convolution fusion | flops 234881024 | bytes 14974976 | tf_op jit(solution)/shard_map/dot_general | solution.py:35
  49.0 0.7 reshape.18
  49.7 5.5 %all-to-all-start = ((f32[8,2,1,1024]{3,1,2,0:T(2,128)}), f32[8,2,1,1024]{3,1,2,0:T(2,128)S(1)}, u32[]{:S(2)}, u32[]{:S(2)}) async-start(f32[8,2,1,1024]{3,1,2,0:T(2,128)} %bitcast.4), calls=%async_computation | async-start | bytes 131072 | tf_op jit(solution)/shard_map/all_to_all | solution.py:45
  55.3 6.8 %all-to-all-done = f32[8,2,1,1024]{3,1,2,0:T(2,128)S(1)} async-done(((f32[8,2,1,1024]{3,1,2,0:T(2,128)}), f32[8,2,1,1024]{3,1,2,0:T(2,128)S(1)}, u32[]{:S(2)}, u32[]{:S(2)}) %all-to-all-start) | async-done | bytes 65568 | tf_op jit(solution)/shard_map/all_to_all | solution.py:45
  62.2 3.8 %all_to_all.27 = f32[1,2,1,8192]{3,2,0,1:T(1,128)S(1)} all-to-all(f32[1,2,1,8192]{3,2,0,1:T(1,128)S(1)} %copy.10), channel_id=1, replica_groups=mesh['groups'=2,'vocab'=8,'mp'=2] {'mp'}, dimensions={1} | all-to-all | bytes 131072 | tf_op jit(solution)/shard_map/all_to_all | solution.py:44
  66.0 0.1 reduce_sum.38
  66.1 0.7 multiply_reduce_fusion
  67.6 19.5 %all-gather.4 = bf16[16,1,8192]{2,1,0:T(2,128)(2,1)S(1)} all-gather(bf16[1,1,8192]{2,1,0:T(2,128)(2,1)S(1)} %convert_bitcast_fusion), channel_id=1, replica_groups=mesh['groups'=2,'vocab'=8,'mp'=2] {'vocab','mp'}, dimensions={0}, use_global_device_ids=true | all-gather | bytes 278528 | tf_op jit(solution)/shard_map/all_gather | solution.py:61
  87.0 0.3 constant_dynamic-slice_fusion.3
  87.3 4.0 %fusion.7 = f32[16,504]{1,0:T(8,128)} fusion(bf16[4096,504]{0,1:T(8,128)(2,1)} %param.14, bf16[16,1,4096]{2,1,0:T(2,128)(2,1)S(1)} %constant_dynamic-slice_fusion.3), kind=kOutput, calls=%fused_computation.11 | convolution fusion | flops 66060288 | bytes 4292096 | tf_op jit(solution)/shard_map/dot_general | solution.py:66
  91.3 0.6 dynamic-slice
  92.6 4.1 %reduce-scatter.2.cloned.1.call-done = f32[8,504]{1,0:T(8,128)} async-done(((f32[16,504]{1,0:T(8,128)}), f32[8,504]{1,0:T(8,128)}) %reduce-scatter.2.cloned.1.call-update) | async-done | bytes 16144 | tf_op jit(solution)/shard_map/reduce_scatter | solution.py:67
  96.8 0.8 reduce_max.9
  97.6 0.2 dynamic-update-slice
  97.8 0.9 select_reduce_fusion
  98.8 0.2 dynamic-update-slice.2
  99.0 0.2 dynamic-update-slice.1
  99.2 21.6 %all-reduce.3 = (f32[64]{0:T(128)S(1)}, f32[64]{0:T(128)S(1)}, f32[64]{0:T(128)S(1)}) all-reduce(f32[64]{0:T(128)S(1)} %dynamic-update-slice, f32[64]{0:T(128)S(1)} %dynamic-update-slice.1, f32[64]{0:T(128)S(1)} %dynamic-update-slice.2), channel_id=2, replica_groups=mesh['groups'=2,'vocab'=8,'mp'=2] {'vocab'}, use_global_device_ids=true, to_apply=%add | all-reduce | flops 192 | bytes 1536
  120.8 0.1 reshape.20
  121.0 0.3 while.19
  121.3 0.5 log_subtract_fusion
  (27 shorter events, 0.6 us)
Async XLA Ops:
  6.5 84.8 %copy-start.3 = (u32[32]{0:T(128)S(1)}, u32[32]{0:T(128)}, u32[]{:S(2)}) copy-start(u32[32]{0:T(128)} %constant.71) | copy-start | bytes 388
  6.5 48.7 %copy-start.1 = (bf16[8192]{0:T(1024)(128)(2,1)S(1)}, bf16[8192]{0:T(1024)(128)(2,1)}, u32[]{:S(2)}) copy-start(bf16[8192]{0:T(1024)(128)(2,1)} %param.13) | copy-start | bytes 49156
  6.5 59.5 %copy-start = (bf16[1,8192]{1,0:T(2,128)(2,1)S(1)}, bf16[1,8192]{1,0:T(2,128)(2,1)}, u32[]{:S(2)}) copy-start(bf16[1,8192]{1,0:T(2,128)(2,1)} %param.12) | copy-start | bytes 49156
  6.5 84.8 %copy-start.2 = (s32[8]{0:T(128)S(1)}, s32[8]{0:T(128)}, u32[]{:S(2)}) copy-start(s32[8]{0:T(128)} %param.15) | copy-start | bytes 100
  49.7 12.4 %all-to-all-start = ((f32[8,2,1,1024]{3,1,2,0:T(2,128)}), f32[8,2,1,1024]{3,1,2,0:T(2,128)S(1)}, u32[]{:S(2)}, u32[]{:S(2)}) async-start(f32[8,2,1,1024]{3,1,2,0:T(2,128)} %bitcast.4), calls=%async_computation | async-start | bytes 131072 | tf_op jit(solution)/shard_map/all_to_all | solution.py:45
  55.2 41.5 %reduce-scatter.2.cloned.1.call-start = ((), (), s32[]{:S(2)}) async-start(), calls=%async_computation.3 | async-start | bytes 49152 | tf_op jit(solution)/shard_map/reduce_scatter | solution.py:67
Sparse Core Ops, SparseCore 0:
  91.4 5.2 reduce-scatter.1
where the time goes:
time: 129 us
  blocking collectives  77.3 us (60%)
  between operations  14.9 us (12%)
  matrix products  13 us (10%)
  waiting for transfers between devices  11 us (9%)
  starting transfers between devices  5.54 us (4%)
  other arithmetic  4.22 us (3%)
  local copies, waits for them, and re-layouts  2.68 us (2%)
    all_gather x1, blocking collectives, body(): lax.all_gather(gated_units, 'vocab', axis=0, tiled=True)  32.5 us
    unnamed x1, blocking collectives  21.6 us
    all_gather x1, blocking collectives, body(): lax.all_gather(normed, ('vocab', 'mp'), axis=0, tiled=True)  19.5 us
    dot_general x1, matrix products, body(): lax.dot_general(lax.all_gather(gated_units, 'vocab', axis=0, tiled=True),...  9.05 us
    all_to_all x1, waiting for transfers between devices, body(): lax.all_to_all(grouped, 'vocab', split_axis=0, concat_axis=3, tiled=True)  6.83 us
    all_to_all x1, starting transfers between devices, body(): lax.all_to_all(grouped, 'vocab', split_axis=0, concat_axis=3, tiled=True)  5.51 us
    reduce_scatter x1, waiting for transfers between devices, body(): lax.psum_scatter(logit_terms, 'mp', scatter_dimension=0, tiled=True)  4.13 us
    dot_general x1, matrix products, body(): jnp.dot(halves, head_weight, preferred_element_type=jnp.float32)  3.98 us
  transfers between devices with their start and end apart: 2, of which 2 were waited for; matrix products, arithmetic and copies ran while one was open for 1% of the time, Pallas kernels for 0%

commit v1 on v0

--- a/solution.py
+++ b/solution.py
@@ -1,6 +1,10 @@
+import functools
+
 import jax
 import jax.numpy as jnp
 from jax import lax
+from jax.experimental import pallas as pl
+from jax.experimental.pallas import tpu as pltpu
 from jax.sharding import PartitionSpec as P
 
 EPSILON = 1e-05
@@ -24,7 +28,7 @@
     return (joint_max, joint_sum, earlier[2] + follows[2])
 
 
-def body(gate_pre, up_pre, down_weight, residual, norm_gain, head_weight, targets):
+def plain_body(gate_pre, up_pre, down_weight, residual, norm_gain, head_weight, targets):
     vocab_count = lax.axis_size("vocab")
     model_count = lax.axis_size("mp")
     model_index = lax.axis_index("mp")
@@ -72,6 +76,489 @@
     exp_total = jnp.sum(jnp.exp(logits - row_top[:, None]), axis=1)
     merged = merged_2((row_top, exp_total, chosen), "vocab", merge_stats)
     return merged[2] - merged[0] - jnp.log(merged[1])
+
+
+GATHER_CHUNKS = 2
+WEIGHT_COLS = 512
+LANES = 128
+
+
+def diagonal(rows):
+    return lax.broadcasted_iota(jnp.int32, (rows, LANES), 0) == lax.broadcasted_iota(
+        jnp.int32, (rows, LANES), 1
+    )
+
+
+def to_lanes(column):
+    rows = column.shape[0]
+    spread = jnp.where(diagonal(rows), jnp.broadcast_to(column, (rows, LANES)), 0.0)
+    return jnp.sum(spread, axis=0, keepdims=True)
+
+
+def to_rows(lanes, rows):
+    spread = jnp.where(diagonal(rows), jnp.broadcast_to(lanes, (rows, LANES)), 0.0)
+    return jnp.sum(spread, axis=1, keepdims=True)
+
+
+def kernel(
+    V,
+    M,
+    targets_ref,
+    gate_hbm,
+    up_hbm,
+    down_hbm,
+    residual_hbm,
+    gain_hbm,
+    head_hbm,
+    out_ref,
+    gate,
+    up,
+    down,
+    own_residual,
+    gain,
+    head,
+    gated_in,
+    gated_rows,
+    gated,
+    residual_out,
+    residual_in,
+    residual_rows,
+    update_out,
+    update_in,
+    stream_out,
+    stream_in,
+    square_in,
+    logits_out,
+    logits_in,
+    stats_in,
+    in_sem,
+    down_sem,
+    gated_send,
+    gated_recv,
+    residual_send,
+    residual_recv,
+    update_sem,
+    stream_send,
+    stream_recv,
+    square_send,
+    square_recv,
+    logits_sem,
+    stats_send,
+    stats_recv,
+):
+    v = lax.axis_index("vocab")
+    m = lax.axis_index("mp")
+    other = 1 - m
+    me = v * M + m
+    N = V * M
+    token_rows, width = gate.shape
+    T = V * token_rows
+    block_cols = down.shape[1]
+    part_cols = block_cols // M
+    weight_chunks, _, weight_cols = down.shape
+    chunks = gated_in.shape[0]
+    chunk_cols = width // chunks
+    own_tokens = T // M
+    vocab_cols = head.shape[1]
+    half_owner = v // (V // M)
+
+    def peer(i):
+        return lax.rem(me + i, N)
+
+    def coords(index):
+        return {"vocab": index // M, "mp": lax.rem(index, M)}
+
+    def remote(src, dst, send, recv, vocab, mp):
+        return pltpu.make_async_remote_copy(
+            src_ref=src,
+            dst_ref=dst,
+            send_sem=send,
+            recv_sem=recv,
+            device_id={"vocab": vocab, "mp": mp},
+            device_id_type=pl.DeviceIdType.MESH,
+        )
+
+    barrier = pltpu.get_barrier_semaphore()
+    for i in range(1, N):
+        pl.semaphore_signal(
+            barrier, inc=1, device_id=coords(peer(i)), device_id_type=pl.DeviceIdType.MESH
+        )
+
+    loads = [
+        pltpu.make_async_copy(gate_hbm, gate, in_sem.at[0]),
+        pltpu.make_async_copy(up_hbm, up, in_sem.at[1]),
+        pltpu.make_async_copy(residual_hbm, own_residual, in_sem.at[2]),
+        pltpu.make_async_copy(gain_hbm, gain, in_sem.at[3]),
+        pltpu.make_async_copy(head_hbm, head, in_sem.at[4]),
+    ]
+    for load in loads[:3]:
+        load.start()
+
+    def down_copy(k):
+        return pltpu.make_async_copy(
+            down_hbm.at[:, pl.ds(pl.multiple_of(k * weight_cols, weight_cols), weight_cols)],
+            down.at[k],
+            down_sem.at[k],
+        )
+
+    for k in range(weight_chunks):
+        down_copy(k).start()
+    loads[4].start()
+    loads[3].start()
+
+    loads[0].wait()
+    loads[1].wait()
+    for a in range(chunks):
+        part = slice(a * chunk_cols, (a + 1) * chunk_cols)
+        g = gate[:, part].astype(jnp.float32)
+        u = up[:, part].astype(jnp.float32)
+        gated_in[a, v] = (jax.nn.silu(g) * u).astype(jnp.bfloat16)
+    loads[2].wait()
+    for n in range(N):
+        residual_out[n] = own_residual[:, n * part_cols : (n + 1) * part_cols].astype(jnp.float32)
+    residual_in[me] = residual_out[me]
+
+    pl.semaphore_wait(barrier, N - 1)
+
+    def gated_copy(a, i):
+        to = lax.rem(v + i, V)
+        return remote(
+            gated_in.at[a, v], gated_in.at[a, v], gated_send.at[a, i], gated_recv.at[a, v], to, m
+        )
+
+    def gated_arrival(a, i):
+        source = lax.rem(v + i, V)
+        return remote(
+            gated_in.at[a, source],
+            gated_in.at[a, source],
+            gated_send.at[a, i],
+            gated_recv.at[a, source],
+            source,
+            m,
+        )
+
+    def residual_copy(i):
+        to = peer(i)
+        return remote(
+            residual_out.at[to],
+            residual_in.at[me],
+            residual_send.at[i],
+            residual_recv.at[me],
+            to // M,
+            lax.rem(to, M),
+        )
+
+    def residual_arrival(i):
+        source = peer(i)
+        return remote(
+            residual_out.at[source],
+            residual_in.at[source],
+            residual_send.at[i],
+            residual_recv.at[source],
+            source // M,
+            lax.rem(source, M),
+        )
+
+    for a in range(chunks):
+        for i in range(1, V):
+            gated_copy(a, i).start()
+    for i in range(1, N):
+        residual_copy(i).start()
+
+    per_chunk = weight_chunks // chunks
+
+    def take_chunk(a):
+        for i in range(1, V):
+            gated_arrival(a, i).wait_recv()
+        for s in range(V):
+            gated_rows[s * token_rows : (s + 1) * token_rows, :] = gated_in[a, s].astype(
+                jnp.float32
+            )
+        for k in range(per_chunk):
+            gated[a * per_chunk + k] = gated_rows[
+                :, k * weight_cols : (k + 1) * weight_cols
+            ].astype(jnp.bfloat16)
+
+    def term(k, which):
+        rows = pl.ds(pl.multiple_of(which * part_cols, part_cols), part_cols)
+        return lax.dot_general(
+            gated[k],
+            down[k, rows, :],
+            (((1,), (1,)), ((), ())),
+            preferred_element_type=jnp.float32,
+        )
+
+    zero = jnp.zeros((T, part_cols), jnp.float32)
+
+    def both(k, sums):
+        down_copy(k).wait()
+        return sums[0] + term(k, other), sums[1] + term(k, m)
+
+    def first(k, total):
+        down_copy(k).wait()
+        return total + term(k, other)
+
+    sums = (zero, zero)
+    for a in range(chunks - 1):
+        take_chunk(a)
+        sums = lax.fori_loop(a * per_chunk, (a + 1) * per_chunk, both, sums)
+    take_chunk(chunks - 1)
+    last = (chunks - 1) * per_chunk
+    update_out[...] = lax.fori_loop(last, weight_chunks, first, sums[0])
+    swap = remote(update_out, update_in, update_sem.at[0], update_sem.at[1], v, other)
+    swap.start()
+    own = lax.fori_loop(last, weight_chunks, lambda k, total: total + term(k, m), sums[1])
+
+    for i in range(1, N):
+        residual_arrival(i).wait_recv()
+    for n in range(N):
+        residual_rows[n : n + 1, :] = residual_in[n]
+    swap.wait_recv()
+    stream = (residual_rows[...] + (own + update_in[...])).astype(jnp.bfloat16)
+    stream_out[...] = stream
+    wide = stream.astype(jnp.float32)
+    square_in[me] = to_lanes(jnp.sum(wide * wide, axis=1, keepdims=True))
+
+    slot = lax.rem(v, V // M) * M + m
+
+    def square_copy(i):
+        to = peer(i)
+        return remote(
+            square_in.at[me],
+            square_in.at[me],
+            square_send.at[i],
+            square_recv.at[me],
+            to // M,
+            lax.rem(to, M),
+        )
+
+    def square_arrival(i):
+        source = peer(i)
+        return remote(
+            square_in.at[source],
+            square_in.at[source],
+            square_send.at[i],
+            square_recv.at[source],
+            source // M,
+            lax.rem(source, M),
+        )
+
+    def stream_copy(i):
+        return remote(
+            stream_out,
+            stream_in.at[slot],
+            stream_send.at[i],
+            stream_recv.at[slot],
+            lax.rem(v + i, V),
+            half_owner,
+        )
+
+    def stream_arrival(j):
+        return remote(
+            stream_out, stream_in.at[j], stream_send.at[0], stream_recv.at[j], v, other
+        )
+
+    for i in range(1, V):
+        stream_copy(i).start()
+
+    @pl.when(m != half_owner)
+    def _():
+        stream_copy(0).start()
+
+    for i in range(1, N):
+        square_copy(i).start()
+
+    @pl.when(m == half_owner)
+    def _():
+        stream_in[slot] = stream
+
+    loads[3].wait()
+    loads[4].wait()
+    for i in range(1, N):
+        square_arrival(i).wait_recv()
+    squares = square_in[0]
+    for n in range(1, N):
+        squares = squares + square_in[n]
+    mean_square = to_rows(squares, T) * (1.0 / (N * part_cols))
+    scale = lax.rsqrt(mean_square + EPSILON)
+
+    slots = stream_in.shape[0]
+    partial = jnp.zeros((T, vocab_cols), jnp.float32)
+    for j in range(slots):
+
+        @pl.when(jnp.logical_or(m != half_owner, slot != j))
+        def _():
+            stream_arrival(j).wait_recv()
+
+        feature = pl.multiple_of(m * (slots * part_cols) + j * part_cols, part_cols)
+        normed = (
+            stream_in[j].astype(jnp.float32)
+            * scale
+            * gain[:, pl.ds(feature, part_cols)].astype(jnp.float32)
+        ).astype(jnp.bfloat16)
+        partial = partial + jnp.dot(
+            normed,
+            head[j * part_cols : (j + 1) * part_cols, :],
+            preferred_element_type=jnp.float32,
+        )
+
+    for n in range(M):
+        logits_out[n] = partial[n * own_tokens : (n + 1) * own_tokens, :]
+    swap_logits = remote(
+        logits_out.at[other], logits_in, logits_sem.at[0], logits_sem.at[1], v, other
+    )
+    swap_logits.start()
+    row = lax.broadcasted_iota(jnp.int32, (own_tokens, vocab_cols), 0)
+    wanted = jnp.zeros((own_tokens, vocab_cols), jnp.int32)
+    for t in range(own_tokens):
+        wanted = jnp.where(row == t, targets_ref[t], wanted)
+    columns = lax.broadcasted_iota(jnp.int32, (own_tokens, vocab_cols), 1) + v * vocab_cols
+    swap_logits.wait_recv()
+    logits = logits_out[m] + logits_in[...]
+    top = jnp.max(logits, axis=1, keepdims=True)
+    total = jnp.sum(jnp.exp(logits - top), axis=1, keepdims=True)
+    chosen = jnp.sum(jnp.where(columns == wanted, logits, 0.0), axis=1, keepdims=True)
+    stats_in[v, :, 0:LANES] = to_lanes(top)
+    stats_in[v, :, LANES : 2 * LANES] = to_lanes(total)
+    stats_in[v, :, 2 * LANES : 3 * LANES] = to_lanes(chosen)
+
+    def stats_copy(i):
+        return remote(
+            stats_in.at[v],
+            stats_in.at[v],
+            stats_send.at[i],
+            stats_recv.at[v],
+            lax.rem(v + i, V),
+            m,
+        )
+
+    def stats_arrival(i):
+        source = lax.rem(v + i, V)
+        return remote(
+            stats_in.at[source],
+            stats_in.at[source],
+            stats_send.at[i],
+            stats_recv.at[source],
+            source,
+            m,
+        )
+
+    for i in range(1, V):
+        stats_copy(i).start()
+    for a in range(chunks):
+        for i in range(1, V):
+            gated_copy(a, i).wait_send()
+    for i in range(1, N):
+        residual_copy(i).wait_send()
+        square_copy(i).wait_send()
+    for i in range(1, V):
+        stream_copy(i).wait_send()
+
+    @pl.when(m != half_owner)
+    def _():
+        stream_copy(0).wait_send()
+
+    swap.wait_send()
+    swap_logits.wait_send()
+    for i in range(1, V):
+        stats_arrival(i).wait_recv()
+    joint = stats_in[0, :, 0:LANES]
+    for n in range(1, V):
+        joint = jnp.maximum(joint, stats_in[n, :, 0:LANES])
+    exp_total = jnp.zeros((1, LANES), jnp.float32)
+    picked = jnp.zeros((1, LANES), jnp.float32)
+    for n in range(V):
+        exp_total = exp_total + stats_in[n, :, LANES : 2 * LANES] * jnp.exp(
+            stats_in[n, :, 0:LANES] - joint
+        )
+        picked = picked + stats_in[n, :, 2 * LANES : 3 * LANES]
+    out_ref[...] = picked - joint - jnp.log(exp_total)
+    for i in range(1, V):
+        stats_copy(i).wait_send()
+
+
+def body(gate_pre, up_pre, down_weight, residual, norm_gain, head_weight, targets):
+    V = lax.axis_size("vocab")
+    M = lax.axis_size("mp")
+    token_rows, width = gate_pre.shape
+    block_cols = down_weight.shape[0]
+    half_width, vocab_cols = head_weight.shape
+    T = V * token_rows
+    fits = (
+        M == 2
+        and V % M == 0
+        and T <= LANES
+        and T % 16 == 0
+        and residual.shape[0] == 1
+        and block_cols % (M * LANES) == 0
+        and width % (GATHER_CHUNKS * WEIGHT_COLS) == 0
+    )
+    if not fits:
+        return plain_body(
+            gate_pre, up_pre, down_weight, residual, norm_gain, head_weight, targets
+        )
+    N = V * M
+    part_cols = block_cols // M
+    weight_chunks = width // WEIGHT_COLS
+    slots = V
+    any_space = pl.BlockSpec(memory_space=pl.ANY)
+    f32, bf16 = jnp.float32, jnp.bfloat16
+    dma = pltpu.SemaphoreType.DMA
+    result = pl.pallas_call(
+        functools.partial(kernel, V, M),
+        out_shape=jax.ShapeDtypeStruct((1, LANES), f32),
+        in_specs=[pl.BlockSpec(memory_space=pltpu.SMEM)] + [any_space] * 6,
+        out_specs=pl.BlockSpec(memory_space=pltpu.VMEM),
+        scratch_shapes=[
+            pltpu.VMEM((token_rows, width), bf16),
+            pltpu.VMEM((token_rows, width), bf16),
+            pltpu.VMEM((weight_chunks, block_cols, WEIGHT_COLS), bf16),
+            pltpu.VMEM(residual.shape, bf16),
+            pltpu.VMEM((1, norm_gain.shape[0]), bf16),
+            pltpu.VMEM(head_weight.shape, bf16),
+            pltpu.VMEM((GATHER_CHUNKS, V, token_rows, width // GATHER_CHUNKS), bf16),
+            pltpu.VMEM((T, width // GATHER_CHUNKS), f32),
+            pltpu.VMEM((weight_chunks, T, WEIGHT_COLS), bf16),
+            pltpu.VMEM((N, 1, part_cols), f32),
+            pltpu.VMEM((N, 1, part_cols), f32),
+            pltpu.VMEM((T, part_cols), f32),
+            pltpu.VMEM((T, part_cols), f32),
+            pltpu.VMEM((T, part_cols), f32),
+            pltpu.VMEM((T, part_cols), bf16),
+            pltpu.VMEM((slots, T, part_cols), bf16),
+            pltpu.VMEM((N, 1, LANES), f32),
+            pltpu.VMEM((M, T // M, vocab_cols), f32),
+            pltpu.VMEM((T // M, vocab_cols), f32),
+            pltpu.VMEM((V, 1, 3 * LANES), f32),
+            dma((5,)),
+            dma((weight_chunks,)),
+            dma((GATHER_CHUNKS, V)),
+            dma((GATHER_CHUNKS, V)),
+            dma((N,)),
+            dma((N,)),
+            dma((2,)),
+            dma((V,)),
+            dma((slots,)),
+            dma((N,)),
+            dma((N,)),
+            dma((2,)),
+            dma((V,)),
+            dma((V,)),
+        ],
+        compiler_params=pltpu.CompilerParams(
+            collective_id=0, has_side_effects=True, vmem_limit_bytes=56 * 1024 * 1024
+        ),
+        name="scored_head",
+    )(
+        targets,
+        gate_pre,
+        up_pre,
+        down_weight,
+        residual,
+        norm_gain.reshape(1, -1),
+        head_weight,
+    )
+    return result[0, : targets.shape[0]]
 
 
 def solution(mesh):

time: 129 us -> 42.5 us (0.33)
  blocking collectives: 77.3 us -> 0 us
  Pallas kernels: 0 us -> 33.3 us
  between operations: 14.9 us -> 0.01 us
  matrix products: 13 us -> 0 us
  waiting for transfers between devices: 11 us -> 0 us
  local copies, waits for them, and re-layouts: 2.68 us -> 8.98 us
  starting transfers between devices: 5.54 us -> 0 us
  other arithmetic: 4.22 us -> 0 us
    all_gather x2 -> x0, blocking collectives: 51.9 us -> none  [the longest x1 32.5 us: body(): lax.all_gather(gated_units, 'vocab', axis=0, tiled=True)]
    pallas_call x0 -> x1, Pallas kernels: none -> 33.3 us  [body(): pl.pallas_call(functools.partial(kernel, V, M), out_shape=jax.ShapeDtypeS...]
    unnamed x1 -> x0, blocking collectives: 21.6 us -> none
    dot_general x2 -> x0, matrix products: 13 us -> none  [the longest x1 9.05 us: body(): lax.dot_general(lax.all_gather(gated_units, 'vocab', axis=0, tiled=True),...]
    all_to_all x1 -> x0, waiting for transfers between devices: 6.83 us -> none  [body(): lax.all_to_all(grouped, 'vocab', split_axis=0, concat_axis=3, tiled=True)]
    all_to_all x1 -> x0, starting transfers between devices: 5.51 us -> none  [body(): lax.all_to_all(grouped, 'vocab', split_axis=0, concat_axis=3, tiled=True)]
    unnamed x16 -> x1, local copies, waits for them, and re-layouts: 1.44 us -> 6.46 us
    reduce_scatter x1 -> x0, waiting for transfers between devices: 4.13 us -> none  [body(): lax.psum_scatter(logit_terms, 'mp', scatter_dimension=0, tiled=True)]
  transfers between devices with their start and end apart: 2 -> 0, of which waited for: 2 -> 0; matrix products, arithmetic and copies ran while one was open for 1% -> 0% of each run, Pallas kernels for 0% -> 0%
where the time goes in v1:
time: 42.5 us; the launch traced here: 42.2 us
  Pallas kernels  33.3 us (78%)
  local copies, waits for them, and re-layouts  8.98 us (21%)
    pallas_call x1, Pallas kernels, body(): pl.pallas_call(functools.partial(kernel, V, M), out_shape=jax.ShapeDtypeS...  33.3 us
    unnamed x1, local copies, waits for them, and re-layouts  6.46 us
    reshape x1, local copies, waits for them, and re-layouts, body(): norm_gain.reshape(1, -1)  1.33 us
    squeeze x1, local copies, waits for them, and re-layouts, body(): return result[0, :targets.shape[0]]  1.19 us

profile of v1, /device:TPU:0, one launch (start us, length us, event | category | flops | bytes accessed | tf_op | source)
XLA Modules:
  0.0 42.2 jit_solution(15254802015273106584)
XLA Ops:
  0.0 1.3 %reshape.3.gain_hbm = bf16[1,8192]{1,0:T(2,128)(2,1)} reshape(bf16[8192]{0:T(1024)(128)(2,1)} %param.11) | data formatting | bytes 32768 | tf_op jit(solution)/shard_map/reshape | solution.py:558
  1.3 6.5 %copy.8.head_hbm = bf16[4096,504]{1,0:T(8,128)(2,1)} copy(bf16[4096,504]{0,1:T(8,128)(2,1)} %param.12) | data formatting | bytes 8257536 | tf_op args[5]
  7.8 33.3 %scored_head.1 = f32[1,128]{1,0:T(1,128)} custom-call(s32[8]{0:T(128)} %targets_ref.1, bf16[2,7168]{1,0:T(2,128)(2,1)} %gate_hbm.1, bf16[2,7168]{1,0:T(2,128)(2,1)} %up_hbm.1, bf16[1024,7168]{1,0:T(8,128)(2,1)} %down_hbm.1, bf16[1,8192]{1,0:T(2,128)(2,1)} %residual_hbm.1, bf16[1,8192]{1,0:T(2,128)(2,1)} %reshape.3.gain_hbm, bf16[4096,504]{1,0:T(8,128)(2,1)} %copy.8.head_hbm), custom_call_target="tpu_custom_call" | custom-call | tf_op jit(solution)/shard_map/scored_head/pallas_call | solution.py:507
  41.1 1.2 %slice_bitcast_fusion = f32[8]{0:T(128)} fusion(f32[1,128]{1,0:T(1,128)} %scored_head.1), kind=kLoop, calls=%fused_computation | loop fusion | bytes 64 | tf_op jit(solution)/shard_map/squeeze | solution.py:561

commit v2 on v1

--- a/solution.py
+++ b/solution.py
@@ -78,8 +78,8 @@
     return merged[2] - merged[0] - jnp.log(merged[1])
 
 
-GATHER_CHUNKS = 2
-WEIGHT_COLS = 512
+GATHER_CHUNKS = 4
+MATRIX_SIDE = 256
 LANES = 128
 
 
@@ -119,7 +119,6 @@
     head,
     gated_in,
     gated_rows,
-    gated,
     residual_out,
     residual_in,
     residual_rows,
@@ -155,11 +154,9 @@
     T = V * token_rows
     block_cols = down.shape[1]
     part_cols = block_cols // M
-    weight_chunks, _, weight_cols = down.shape
-    chunks = gated_in.shape[0]
-    chunk_cols = width // chunks
+    chunks, _, chunk_cols = down.shape
     own_tokens = T // M
-    vocab_cols = head.shape[1]
+    vocab_cols = head.shape[0]
     half_owner = v // (V // M)
 
     def peer(i):
@@ -188,7 +185,11 @@
         pltpu.make_async_copy(gate_hbm, gate, in_sem.at[0]),
         pltpu.make_async_copy(up_hbm, up, in_sem.at[1]),
         pltpu.make_async_copy(residual_hbm, own_residual, in_sem.at[2]),
-        pltpu.make_async_copy(gain_hbm, gain, in_sem.at[3]),
+        pltpu.make_async_copy(
+            gain_hbm.at[pl.ds(pl.multiple_of(m * gain.shape[0], gain.shape[0]), gain.shape[0])],
+            gain,
+            in_sem.at[3],
+        ),
         pltpu.make_async_copy(head_hbm, head, in_sem.at[4]),
     ]
     for load in loads[:3]:
@@ -196,12 +197,12 @@
 
     def down_copy(k):
         return pltpu.make_async_copy(
-            down_hbm.at[:, pl.ds(pl.multiple_of(k * weight_cols, weight_cols), weight_cols)],
+            down_hbm.at[:, pl.ds(pl.multiple_of(k * chunk_cols, chunk_cols), chunk_cols)],
             down.at[k],
             down_sem.at[k],
         )
 
-    for k in range(weight_chunks):
+    for k in range(chunks):
         down_copy(k).start()
     loads[4].start()
     loads[3].start()
@@ -265,8 +266,6 @@
     for i in range(1, N):
         residual_copy(i).start()
 
-    per_chunk = weight_chunks // chunks
-
     def take_chunk(a):
         for i in range(1, V):
             gated_arrival(a, i).wait_recv()
@@ -274,40 +273,28 @@
             gated_rows[s * token_rows : (s + 1) * token_rows, :] = gated_in[a, s].astype(
                 jnp.float32
             )
-        for k in range(per_chunk):
-            gated[a * per_chunk + k] = gated_rows[
-                :, k * weight_cols : (k + 1) * weight_cols
-            ].astype(jnp.bfloat16)
-
-    def term(k, which):
+        return gated_rows[...].astype(jnp.bfloat16)
+
+    def term(gated, a, which):
         rows = pl.ds(pl.multiple_of(which * part_cols, part_cols), part_cols)
         return lax.dot_general(
-            gated[k],
-            down[k, rows, :],
+            gated,
+            down[a, rows, :],
             (((1,), (1,)), ((), ())),
             preferred_element_type=jnp.float32,
         )
 
-    zero = jnp.zeros((T, part_cols), jnp.float32)
-
-    def both(k, sums):
-        down_copy(k).wait()
-        return sums[0] + term(k, other), sums[1] + term(k, m)
-
-    def first(k, total):
-        down_copy(k).wait()
-        return total + term(k, other)
-
-    sums = (zero, zero)
-    for a in range(chunks - 1):
-        take_chunk(a)
-        sums = lax.fori_loop(a * per_chunk, (a + 1) * per_chunk, both, sums)
-    take_chunk(chunks - 1)
-    last = (chunks - 1) * per_chunk
-    update_out[...] = lax.fori_loop(last, weight_chunks, first, sums[0])
-    swap = remote(update_out, update_in, update_sem.at[0], update_sem.at[1], v, other)
-    swap.start()
-    own = lax.fori_loop(last, weight_chunks, lambda k, total: total + term(k, m), sums[1])
+    theirs = jnp.zeros((T, part_cols), jnp.float32)
+    own = theirs
+    for a in range(chunks):
+        gated = take_chunk(a)
+        down_copy(a).wait()
+        theirs = theirs + term(gated, a, other)
+        if a == chunks - 1:
+            update_out[...] = theirs
+            swap = remote(update_out, update_in, update_sem.at[0], update_sem.at[1], v, other)
+            swap.start()
+        own = own + term(gated, a, m)
 
     for i in range(1, N):
         residual_arrival(i).wait_recv()
@@ -358,15 +345,14 @@
             stream_out, stream_in.at[j], stream_send.at[0], stream_recv.at[j], v, other
         )
 
+    for i in range(1, N):
+        square_copy(i).start()
     for i in range(1, V):
         stream_copy(i).start()
 
     @pl.when(m != half_owner)
     def _():
         stream_copy(0).start()
-
-    for i in range(1, N):
-        square_copy(i).start()
 
     @pl.when(m == half_owner)
     def _():
@@ -383,6 +369,7 @@
     scale = lax.rsqrt(mean_square + EPSILON)
 
     slots = stream_in.shape[0]
+    gains = gain[...].astype(jnp.float32)
     partial = jnp.zeros((T, vocab_cols), jnp.float32)
     for j in range(slots):
 
@@ -390,15 +377,19 @@
         def _():
             stream_arrival(j).wait_recv()
 
-        feature = pl.multiple_of(m * (slots * part_cols) + j * part_cols, part_cols)
+        group = part_cols // LANES
+        slot_gain = jnp.concatenate(
+            [gains[j * group + q : j * group + q + 1] for q in range(group)], axis=1
+        )
         normed = (
             stream_in[j].astype(jnp.float32)
             * scale
-            * gain[:, pl.ds(feature, part_cols)].astype(jnp.float32)
+            * slot_gain
         ).astype(jnp.bfloat16)
-        partial = partial + jnp.dot(
+        partial = partial + lax.dot_general(
             normed,
-            head[j * part_cols : (j + 1) * part_cols, :],
+            head[:, j * part_cols : (j + 1) * part_cols],
+            (((1,), (1,)), ((), ())),
             preferred_element_type=jnp.float32,
         )
 
@@ -491,7 +482,8 @@
         and T % 16 == 0
         and residual.shape[0] == 1
         and block_cols % (M * LANES) == 0
-        and width % (GATHER_CHUNKS * WEIGHT_COLS) == 0
+        and width % (GATHER_CHUNKS * MATRIX_SIDE) == 0
+        and half_width % (16 * LANES) == 0
     )
     if not fits:
         return plain_body(
@@ -499,7 +491,7 @@
         )
     N = V * M
     part_cols = block_cols // M
-    weight_chunks = width // WEIGHT_COLS
+    chunk_cols = width // GATHER_CHUNKS
     slots = V
     any_space = pl.BlockSpec(memory_space=pl.ANY)
     f32, bf16 = jnp.float32, jnp.bfloat16
@@ -512,13 +504,12 @@
         scratch_shapes=[
             pltpu.VMEM((token_rows, width), bf16),
             pltpu.VMEM((token_rows, width), bf16),
-            pltpu.VMEM((weight_chunks, block_cols, WEIGHT_COLS), bf16),
+            pltpu.VMEM((GATHER_CHUNKS, block_cols, chunk_cols), bf16),
             pltpu.VMEM(residual.shape, bf16),
-            pltpu.VMEM((1, norm_gain.shape[0]), bf16),
-            pltpu.VMEM(head_weight.shape, bf16),
-            pltpu.VMEM((GATHER_CHUNKS, V, token_rows, width // GATHER_CHUNKS), bf16),
-            pltpu.VMEM((T, width // GATHER_CHUNKS), f32),
-            pltpu.VMEM((weight_chunks, T, WEIGHT_COLS), bf16),
+            pltpu.VMEM((half_width // LANES, LANES), bf16),
+            pltpu.VMEM((vocab_cols, half_width), bf16),
+            pltpu.VMEM((GATHER_CHUNKS, V, token_rows, chunk_cols), bf16),
+            pltpu.VMEM((T, chunk_cols), f32),
             pltpu.VMEM((N, 1, part_cols), f32),
             pltpu.VMEM((N, 1, part_cols), f32),
             pltpu.VMEM((T, part_cols), f32),
@@ -531,7 +522,7 @@
             pltpu.VMEM((T // M, vocab_cols), f32),
             pltpu.VMEM((V, 1, 3 * LANES), f32),
             dma((5,)),
-            dma((weight_chunks,)),
+            dma((GATHER_CHUNKS,)),
             dma((GATHER_CHUNKS, V)),
             dma((GATHER_CHUNKS, V)),
             dma((N,)),
@@ -555,8 +546,8 @@
         up_pre,
         down_weight,
         residual,
-        norm_gain.reshape(1, -1),
-        head_weight,
+        norm_gain.reshape(-1, LANES),
+        head_weight.T,
     )
     return result[0, : targets.shape[0]]
 

time: 42.5 us -> 30.9 us (0.73)
  local copies, waits for them, and re-layouts: 8.98 us -> 1.19 us
  Pallas kernels: 33.3 us -> 29.6 us
    unnamed x1 -> x0, local copies, waits for them, and re-layouts: 6.46 us -> none
    pallas_call x1, Pallas kernels: 33.3 us -> 29.6 us  [body(): pl.pallas_call(functools.partial(kernel, V, M), out_shape=jax.ShapeDtypeS...]
    reshape x1 -> x0, local copies, waits for them, and re-layouts: 1.33 us -> none  [body(): norm_gain.reshape(1, -1)]
where the time goes in v2:
time: 30.9 us; the launch traced here: 30.8 us
  Pallas kernels  29.6 us (96%)
  local copies, waits for them, and re-layouts  1.19 us (4%)
    pallas_call x1, Pallas kernels, body(): pl.pallas_call(functools.partial(kernel, V, M), out_shape=jax.ShapeDtypeS...  29.6 us
    squeeze x1, local copies, waits for them, and re-layouts, body(): return result[0, :targets.shape[0]]  1.19 us

profile of v2, /device:TPU:0, one launch (start us, length us, event | category | flops | bytes accessed | tf_op | source)
XLA Modules:
  0.0 30.8 jit_solution(14747591008701745399)
XLA Ops:
  0.0 29.6 %scored_head.1 = f32[1,128]{1,0:T(1,128)} custom-call(s32[8]{0:T(128)} %targets_ref.1, bf16[2,7168]{1,0:T(2,128)(2,1)} %gate_hbm.1, bf16[2,7168]{1,0:T(2,128)(2,1)} %up_hbm.1, bf16[1024,7168]{1,0:T(8,128)(2,1)} %down_hbm.1, bf16[1,8192]{1,0:T(2,128)(2,1)} %residual_hbm.1, bf16[64,128]{1,0:T(8,128)(2,1)} %bitcast.5, bf16[504,4096]{1,0:T(8,128)(2,1)} %bitcast.4), custom_call_target="tpu_custom_call" | custom-call | tf_op jit(solution)/shard_map/scored_head/pallas_call | solution.py:499
  29.6 1.2 %slice_bitcast_fusion = f32[8]{0:T(128)} fusion(f32[1,128]{1,0:T(1,128)} %scored_head.1), kind=kLoop, calls=%fused_computation | loop fusion | bytes 64 | tf_op jit(solution)/shard_map/squeeze | solution.py:552

commit v3 on v2

--- a/solution.py
+++ b/solution.py
@@ -278,20 +278,20 @@
     def term(gated, a, which):
         rows = pl.ds(pl.multiple_of(which * part_cols, part_cols), part_cols)
         return lax.dot_general(
+            down[a, rows, :],
             gated,
-            down[a, rows, :],
             (((1,), (1,)), ((), ())),
             preferred_element_type=jnp.float32,
         )
 
-    theirs = jnp.zeros((T, part_cols), jnp.float32)
+    theirs = jnp.zeros((part_cols, T), jnp.float32)
     own = theirs
     for a in range(chunks):
         gated = take_chunk(a)
         down_copy(a).wait()
         theirs = theirs + term(gated, a, other)
         if a == chunks - 1:
-            update_out[...] = theirs
+            update_out[...] = theirs.T
             swap = remote(update_out, update_in, update_sem.at[0], update_sem.at[1], v, other)
             swap.start()
         own = own + term(gated, a, m)
@@ -301,7 +301,7 @@
     for n in range(N):
         residual_rows[n : n + 1, :] = residual_in[n]
     swap.wait_recv()
-    stream = (residual_rows[...] + (own + update_in[...])).astype(jnp.bfloat16)
+    stream = (residual_rows[...] + (own.T + update_in[...])).astype(jnp.bfloat16)
     stream_out[...] = stream
     wide = stream.astype(jnp.float32)
     square_in[me] = to_lanes(jnp.sum(wide * wide, axis=1, keepdims=True))
@@ -370,7 +370,7 @@
 
     slots = stream_in.shape[0]
     gains = gain[...].astype(jnp.float32)
-    partial = jnp.zeros((T, vocab_cols), jnp.float32)
+    partial = jnp.zeros((vocab_cols, T), jnp.float32)
     for j in range(slots):
 
         @pl.when(jnp.logical_or(m != half_owner, slot != j))
@@ -387,14 +387,15 @@
             * slot_gain
         ).astype(jnp.bfloat16)
         partial = partial + lax.dot_general(
+            head[:, j * part_cols : (j + 1) * part_cols],
             normed,
-            head[:, j * part_cols : (j + 1) * part_cols],
             (((1,), (1,)), ((), ())),
             preferred_element_type=jnp.float32,
         )
 
+    logits_t = partial.T
     for n in range(M):
-        logits_out[n] = partial[n * own_tokens : (n + 1) * own_tokens, :]
+        logits_out[n] = logits_t[n * own_tokens : (n + 1) * own_tokens, :]
     swap_logits = remote(
         logits_out.at[other], logits_in, logits_sem.at[0], logits_sem.at[1], v, other
     )

time: 30.9 us -> 33.5 us (1.084)
  Pallas kernels: 29.6 us -> 32.1 us
    pallas_call x1, Pallas kernels: 29.6 us -> 32.1 us  [body(): pl.pallas_call(functools.partial(kernel, V, M), out_shape=jax.ShapeDtypeS...]
where the time goes in v3:
time: 33.5 us; the launch traced here: 33.3 us
  Pallas kernels  32.1 us (96%)
  local copies, waits for them, and re-layouts  1.19 us (4%)
    pallas_call x1, Pallas kernels, body(): pl.pallas_call(functools.partial(kernel, V, M), out_shape=jax.ShapeDtypeS...  32.1 us
    squeeze x1, local copies, waits for them, and re-layouts, body(): return result[0, :targets.shape[0]]  1.19 us

profile of v3, /device:TPU:0, one launch (start us, length us, event | category | flops | bytes accessed | tf_op | source)
XLA Modules:
  0.0 33.3 jit_solution(2183285193344287285)
XLA Ops:
  0.0 32.1 %scored_head.1 = f32[1,128]{1,0:T(1,128)} custom-call(s32[8]{0:T(128)} %targets_ref.1, bf16[2,7168]{1,0:T(2,128)(2,1)} %gate_hbm.1, bf16[2,7168]{1,0:T(2,128)(2,1)} %up_hbm.1, bf16[1024,7168]{1,0:T(8,128)(2,1)} %down_hbm.1, bf16[1,8192]{1,0:T(2,128)(2,1)} %residual_hbm.1, bf16[64,128]{1,0:T(8,128)(2,1)} %bitcast.5, bf16[504,4096]{1,0:T(8,128)(2,1)} %bitcast.4), custom_call_target="tpu_custom_call" | custom-call | tf_op jit(solution)/shard_map/scored_head/pallas_call | solution.py:500
  32.1 1.2 %slice_bitcast_fusion = f32[8]{0:T(128)} fusion(f32[1,128]{1,0:T(1,128)} %scored_head.1), kind=kLoop, calls=%fused_computation | loop fusion | bytes 64 | tf_op jit(solution)/shard_map/squeeze | solution.py:553

commit v4 on v2

--- a/solution.py
+++ b/solution.py
@@ -116,6 +116,7 @@
     down,
     own_residual,
     gain,
+    gain_rows,
     head,
     gated_in,
     gated_rows,
@@ -207,6 +208,45 @@
     loads[4].start()
     loads[3].start()
 
+    def gated_copy(a, i):
+        to = lax.rem(v + i, V)
+        return remote(
+            gated_in.at[a, v], gated_in.at[a, v], gated_send.at[a, i], gated_recv.at[a, v], to, m
+        )
+
+    def gated_arrival(a, i):
+        source = lax.rem(v + i, V)
+        return remote(
+            gated_in.at[a, source],
+            gated_in.at[a, source],
+            gated_send.at[a, i],
+            gated_recv.at[a, source],
+            source,
+            m,
+        )
+
+    def residual_copy(i):
+        to = peer(i)
+        return remote(
+            residual_out.at[to],
+            residual_in.at[me],
+            residual_send.at[i],
+            residual_recv.at[me],
+            to // M,
+            lax.rem(to, M),
+        )
+
+    def residual_arrival(i):
+        source = peer(i)
+        return remote(
+            residual_out.at[source],
+            residual_in.at[source],
+            residual_send.at[i],
+            residual_recv.at[source],
+            source // M,
+            lax.rem(source, M),
+        )
+
     loads[0].wait()
     loads[1].wait()
     for a in range(chunks):
@@ -214,66 +254,28 @@
         g = gate[:, part].astype(jnp.float32)
         u = up[:, part].astype(jnp.float32)
         gated_in[a, v] = (jax.nn.silu(g) * u).astype(jnp.bfloat16)
+        if a == 0:
+            pl.semaphore_wait(barrier, N - 1)
+        for i in range(1, V):
+            gated_copy(a, i).start()
     loads[2].wait()
     for n in range(N):
         residual_out[n] = own_residual[:, n * part_cols : (n + 1) * part_cols].astype(jnp.float32)
     residual_in[me] = residual_out[me]
-
-    pl.semaphore_wait(barrier, N - 1)
-
-    def gated_copy(a, i):
-        to = lax.rem(v + i, V)
-        return remote(
-            gated_in.at[a, v], gated_in.at[a, v], gated_send.at[a, i], gated_recv.at[a, v], to, m
-        )
-
-    def gated_arrival(a, i):
-        source = lax.rem(v + i, V)
-        return remote(
-            gated_in.at[a, source],
-            gated_in.at[a, source],
-            gated_send.at[a, i],
-            gated_recv.at[a, source],
-            source,
-            m,
-        )
-
-    def residual_copy(i):
-        to = peer(i)
-        return remote(
-            residual_out.at[to],
-            residual_in.at[me],
-            residual_send.at[i],
-            residual_recv.at[me],
-            to // M,
-            lax.rem(to, M),
-        )
-
-    def residual_arrival(i):
-        source = peer(i)
-        return remote(
-            residual_out.at[source],
-            residual_in.at[source],
-            residual_send.at[i],
-            residual_recv.at[source],
-            source // M,
-            lax.rem(source, M),
-        )
-
-    for a in range(chunks):
-        for i in range(1, V):
-            gated_copy(a, i).start()
     for i in range(1, N):
         residual_copy(i).start()
 
-    def take_chunk(a):
+    def await_chunk(a):
         for i in range(1, V):
             gated_arrival(a, i).wait_recv()
+        down_copy(a).wait()
+
+    def token_chunk(a):
         for s in range(V):
-            gated_rows[s * token_rows : (s + 1) * token_rows, :] = gated_in[a, s].astype(
+            gated_rows[a % 2, s * token_rows : (s + 1) * token_rows, :] = gated_in[a, s].astype(
                 jnp.float32
             )
-        return gated_rows[...].astype(jnp.bfloat16)
+        return gated_rows[a % 2].astype(jnp.bfloat16)
 
     def term(gated, a, which):
         rows = pl.ds(pl.multiple_of(which * part_cols, part_cols), part_cols)
@@ -286,16 +288,30 @@
 
     theirs = jnp.zeros((T, part_cols), jnp.float32)
     own = theirs
+    await_chunk(0)
+    gated = token_chunk(0)
     for a in range(chunks):
-        gated = take_chunk(a)
-        down_copy(a).wait()
         theirs = theirs + term(gated, a, other)
         if a == chunks - 1:
             update_out[...] = theirs
             swap = remote(update_out, update_in, update_sem.at[0], update_sem.at[1], v, other)
             swap.start()
-        own = own + term(gated, a, m)
-
+            own = own + term(gated, a, m)
+        else:
+            await_chunk(a + 1)
+            following = token_chunk(a + 1)
+            own = own + term(gated, a, m)
+            gated = following
+
+    loads[3].wait()
+    loads[4].wait()
+    group = part_cols // LANES
+    gains = gain[...].astype(jnp.float32)
+    for j in range(V):
+        for q in range(group):
+            gain_rows[j, :, q * LANES : (q + 1) * LANES] = gains[
+                j * group + q : j * group + q + 1
+            ]
     for i in range(1, N):
         residual_arrival(i).wait_recv()
     for n in range(N):
@@ -330,15 +346,29 @@
             lax.rem(source, M),
         )
 
-    def stream_copy(i):
+    quarter = V // M
+
+    def stream_copy(i, h):
+        to = lax.rem(v + i, quarter) + h * quarter
         return remote(
             stream_out,
             stream_in.at[slot],
-            stream_send.at[i],
+            stream_send.at[h * quarter + i],
             stream_recv.at[slot],
-            lax.rem(v + i, V),
+            to,
             half_owner,
         )
+
+    def over_stream(act):
+        for i in range(quarter):
+            for h in range(M):
+                if i:
+                    act(stream_copy(i, h))
+                else:
+
+                    @pl.when(jnp.logical_or(h != half_owner, m != half_owner))
+                    def _():
+                        act(stream_copy(i, h))
 
     def stream_arrival(j):
         return remote(
@@ -347,19 +377,12 @@
 
     for i in range(1, N):
         square_copy(i).start()
-    for i in range(1, V):
-        stream_copy(i).start()
-
-    @pl.when(m != half_owner)
-    def _():
-        stream_copy(0).start()
+    over_stream(lambda copy: copy.start())
 
     @pl.when(m == half_owner)
     def _():
         stream_in[slot] = stream
 
-    loads[3].wait()
-    loads[4].wait()
     for i in range(1, N):
         square_arrival(i).wait_recv()
     squares = square_in[0]
@@ -368,30 +391,29 @@
     mean_square = to_rows(squares, T) * (1.0 / (N * part_cols))
     scale = lax.rsqrt(mean_square + EPSILON)
 
-    slots = stream_in.shape[0]
-    gains = gain[...].astype(jnp.float32)
     partial = jnp.zeros((T, vocab_cols), jnp.float32)
-    for j in range(slots):
-
-        @pl.when(jnp.logical_or(m != half_owner, slot != j))
-        def _():
-            stream_arrival(j).wait_recv()
-
-        group = part_cols // LANES
-        slot_gain = jnp.concatenate(
-            [gains[j * group + q : j * group + q + 1] for q in range(group)], axis=1
-        )
-        normed = (
-            stream_in[j].astype(jnp.float32)
-            * scale
-            * slot_gain
-        ).astype(jnp.bfloat16)
-        partial = partial + lax.dot_general(
-            normed,
-            head[:, j * part_cols : (j + 1) * part_cols],
-            (((1,), (1,)), ((), ())),
-            preferred_element_type=jnp.float32,
-        )
+    for i in range(quarter):
+        source = lax.rem(v + quarter - i, quarter)
+        for c in range(M):
+            j = source * M + c
+            if i:
+                stream_arrival(j).wait_recv()
+            else:
+
+                @pl.when(jnp.logical_or(m != half_owner, m != c))
+                def _():
+                    stream_arrival(j).wait_recv()
+
+            normed = (stream_in[j].astype(jnp.float32) * scale * gain_rows[j]).astype(
+                jnp.bfloat16
+            )
+            features = pl.ds(pl.multiple_of(j * part_cols, part_cols), part_cols)
+            partial = partial + lax.dot_general(
+                normed,
+                head[:, features],
+                (((1,), (1,)), ((), ())),
+                preferred_element_type=jnp.float32,
+            )
 
     for n in range(M):
         logits_out[n] = partial[n * own_tokens : (n + 1) * own_tokens, :]
@@ -442,12 +464,7 @@
     for i in range(1, N):
         residual_copy(i).wait_send()
         square_copy(i).wait_send()
-    for i in range(1, V):
-        stream_copy(i).wait_send()
-
-    @pl.when(m != half_owner)
-    def _():
-        stream_copy(0).wait_send()
+    over_stream(lambda copy: copy.wait_send())
 
     swap.wait_send()
     swap_logits.wait_send()
@@ -507,9 +524,10 @@
             pltpu.VMEM((GATHER_CHUNKS, block_cols, chunk_cols), bf16),
             pltpu.VMEM(residual.shape, bf16),
             pltpu.VMEM((half_width // LANES, LANES), bf16),
+            pltpu.VMEM((slots, 1, part_cols), f32),
             pltpu.VMEM((vocab_cols, half_width), bf16),
             pltpu.VMEM((GATHER_CHUNKS, V, token_rows, chunk_cols), bf16),
-            pltpu.VMEM((T, chunk_cols), f32),
+            pltpu.VMEM((2, T, chunk_cols), f32),
             pltpu.VMEM((N, 1, part_cols), f32),
             pltpu.VMEM((N, 1, part_cols), f32),
             pltpu.VMEM((T, part_cols), f32),

time: 30.9 us -> 30.9 us (level)
  no operation moved by 1% of the time
where the time goes in v4:
time: 30.9 us; the launch traced here: 30.7 us
  Pallas kernels  29.5 us (95%)
  local copies, waits for them, and re-layouts  1.19 us (4%)
    pallas_call x1, Pallas kernels, body(): pl.pallas_call(functools.partial(kernel, V, M), out_shape=jax.ShapeDtypeS...  29.5 us
    squeeze x1, local copies, waits for them, and re-layouts, body(): return result[0, :targets.shape[0]]  1.19 us

profile of v4, /device:TPU:0, one launch (start us, length us, event | category | flops | bytes accessed | tf_op | source)
XLA Modules:
  0.0 30.7 jit_solution(4218304886638208236)
XLA Ops:
  0.0 29.5 %scored_head.1 = f32[1,128]{1,0:T(1,128)} custom-call(s32[8]{0:T(128)} %targets_ref.1, bf16[2,7168]{1,0:T(2,128)(2,1)} %gate_hbm.1, bf16[2,7168]{1,0:T(2,128)(2,1)} %up_hbm.1, bf16[1024,7168]{1,0:T(8,128)(2,1)} %down_hbm.1, bf16[1,8192]{1,0:T(2,128)(2,1)} %residual_hbm.1, bf16[64,128]{1,0:T(8,128)(2,1)} %bitcast.5, bf16[504,4096]{1,0:T(8,128)(2,1)} %bitcast.4), custom_call_target="tpu_custom_call" | custom-call | tf_op jit(solution)/shard_map/scored_head/pallas_call | solution.py:516
  29.6 1.2 %slice_bitcast_fusion = f32[8]{0:T(128)} fusion(f32[1,128]{1,0:T(1,128)} %scored_head.1), kind=kLoop, calls=%fused_computation | loop fusion | bytes 64 | tf_op jit(solution)/shard_map/squeeze | solution.py:570

commit v5 on v4

--- a/solution.py
+++ b/solution.py
@@ -208,22 +208,38 @@
     loads[4].start()
     loads[3].start()
 
-    def gated_copy(a, i):
-        to = lax.rem(v + i, V)
-        return remote(
-            gated_in.at[a, v], gated_in.at[a, v], gated_send.at[a, i], gated_recv.at[a, v], to, m
-        )
-
-    def gated_arrival(a, i):
-        source = lax.rem(v + i, V)
+    beside = v + 1 - 2 * lax.rem(v, 2)
+    column = V // 2
+
+    def gated_copy(a, source, to, send):
         return remote(
             gated_in.at[a, source],
             gated_in.at[a, source],
-            gated_send.at[a, i],
+            gated_send.at[a, send],
             gated_recv.at[a, source],
-            source,
+            to,
             m,
         )
+
+    def in_column(i):
+        return lax.rem(v + 2 * i, V)
+
+    def across(i):
+        return lax.rem(beside + 2 * i, V)
+
+    def gated_sends(a):
+        return [gated_copy(a, v, in_column(i), i) for i in range(1, column)] + [
+            gated_copy(a, v, beside, 0)
+        ]
+
+    def gated_relays(a):
+        return [gated_copy(a, in_column(i), beside, column + i) for i in range(1, column)]
+
+    def relay_chunk(a):
+        for i in range(1, column):
+            gated_copy(a, in_column(i), in_column(i), 0).wait_recv()
+        for copy in gated_relays(a):
+            copy.start()
 
     def residual_copy(i):
         to = peer(i)
@@ -256,8 +272,8 @@
         gated_in[a, v] = (jax.nn.silu(g) * u).astype(jnp.bfloat16)
         if a == 0:
             pl.semaphore_wait(barrier, N - 1)
-        for i in range(1, V):
-            gated_copy(a, i).start()
+        for copy in gated_sends(a):
+            copy.start()
     loads[2].wait()
     for n in range(N):
         residual_out[n] = own_residual[:, n * part_cols : (n + 1) * part_cols].astype(jnp.float32)
@@ -266,8 +282,8 @@
         residual_copy(i).start()
 
     def await_chunk(a):
-        for i in range(1, V):
-            gated_arrival(a, i).wait_recv()
+        for i in range(column):
+            gated_copy(a, across(i), beside, 0).wait_recv()
         down_copy(a).wait()
 
     def token_chunk(a):
@@ -288,6 +304,9 @@
 
     theirs = jnp.zeros((T, part_cols), jnp.float32)
     own = theirs
+    relay_chunk(0)
+    if chunks > 1:
+        relay_chunk(1)
     await_chunk(0)
     gated = token_chunk(0)
     for a in range(chunks):
@@ -298,6 +317,8 @@
             swap.start()
             own = own + term(gated, a, m)
         else:
+            if a + 2 < chunks:
+                relay_chunk(a + 2)
             await_chunk(a + 1)
             following = token_chunk(a + 1)
             own = own + term(gated, a, m)
@@ -348,19 +369,21 @@
 
     quarter = V // M
 
+    steps = quarter // 2
+
     def stream_copy(i, h):
-        to = lax.rem(v + i, quarter) + h * quarter
+        to = lax.rem(v + 2 * i, quarter) + h * quarter
         return remote(
             stream_out,
             stream_in.at[slot],
-            stream_send.at[h * quarter + i],
+            stream_send.at[h * steps + i],
             stream_recv.at[slot],
             to,
             half_owner,
         )
 
     def over_stream(act):
-        for i in range(quarter):
+        for i in range(steps):
             for h in range(M):
                 if i:
                     act(stream_copy(i, h))
@@ -370,9 +393,23 @@
                     def _():
                         act(stream_copy(i, h))
 
+    def slot_from(base, i, c):
+        return lax.rem(lax.rem(base, quarter) + quarter - 2 * i, quarter) * M + c
+
     def stream_arrival(j):
         return remote(
             stream_out, stream_in.at[j], stream_send.at[0], stream_recv.at[j], v, other
+        )
+
+    def stream_relay(i, c):
+        j = slot_from(v, i, c)
+        return remote(
+            stream_in.at[j],
+            stream_in.at[j],
+            stream_send.at[column + i * M + c],
+            stream_recv.at[j],
+            beside,
+            m,
         )
 
     for i in range(1, N):
@@ -382,6 +419,18 @@
     @pl.when(m == half_owner)
     def _():
         stream_in[slot] = stream
+
+    for i in range(steps):
+        for c in range(M):
+            if i:
+                stream_arrival(slot_from(v, i, c)).wait_recv()
+            else:
+
+                @pl.when(jnp.logical_or(m != half_owner, m != c))
+                def _():
+                    stream_arrival(slot_from(v, i, c)).wait_recv()
+
+            stream_relay(i, c).start()
 
     for i in range(1, N):
         square_arrival(i).wait_recv()
@@ -392,18 +441,11 @@
     scale = lax.rsqrt(mean_square + EPSILON)
 
     partial = jnp.zeros((T, vocab_cols), jnp.float32)
-    for i in range(quarter):
-        source = lax.rem(v + quarter - i, quarter)
-        for c in range(M):
-            j = source * M + c
-            if i:
+    for base in (v, beside):
+        for i, c in [(i, c) for i in range(steps) for c in range(M)]:
+            j = slot_from(base, i, c)
+            if base is beside:
                 stream_arrival(j).wait_recv()
-            else:
-
-                @pl.when(jnp.logical_or(m != half_owner, m != c))
-                def _():
-                    stream_arrival(j).wait_recv()
-
             normed = (stream_in[j].astype(jnp.float32) * scale * gain_rows[j]).astype(
                 jnp.bfloat16
             )
@@ -459,12 +501,15 @@
     for i in range(1, V):
         stats_copy(i).start()
     for a in range(chunks):
-        for i in range(1, V):
-            gated_copy(a, i).wait_send()
+        for copy in gated_sends(a) + gated_relays(a):
+            copy.wait_send()
     for i in range(1, N):
         residual_copy(i).wait_send()
         square_copy(i).wait_send()
     over_stream(lambda copy: copy.wait_send())
+    for i in range(steps):
+        for c in range(M):
+            stream_relay(i, c).wait_send()
 
     swap.wait_send()
     swap_logits.wait_send()
@@ -494,7 +539,7 @@
     T = V * token_rows
     fits = (
         M == 2
-        and V % M == 0
+        and V % (2 * M) == 0
         and T <= LANES
         and T % 16 == 0
         and residual.shape[0] == 1

time: 30.9 us -> 34.1 us (1.10)
  Pallas kernels: 29.5 us -> 32.7 us
    pallas_call x1, Pallas kernels: 29.5 us -> 32.7 us  [body(): pl.pallas_call(functools.partial(kernel, V, M), out_shape=jax.ShapeDtypeS...]
where the time goes in v5:
time: 34.1 us; the launch traced here: 33.9 us
  Pallas kernels  32.7 us (96%)
  local copies, waits for them, and re-layouts  1.19 us (3%)
    pallas_call x1, Pallas kernels, body(): pl.pallas_call(functools.partial(kernel, V, M), out_shape=jax.ShapeDtypeS...  32.7 us
    squeeze x1, local copies, waits for them, and re-layouts, body(): return result[0, :targets.shape[0]]  1.19 us

profile of v5, /device:TPU:0, one launch (start us, length us, event | category | flops | bytes accessed | tf_op | source)
XLA Modules:
  0.0 33.9 jit_solution(10922683945236991881)
XLA Ops:
  0.0 32.7 %scored_head.1 = f32[1,128]{1,0:T(1,128)} custom-call(s32[8]{0:T(128)} %targets_ref.1, bf16[2,7168]{1,0:T(2,128)(2,1)} %gate_hbm.1, bf16[2,7168]{1,0:T(2,128)(2,1)} %up_hbm.1, bf16[1024,7168]{1,0:T(8,128)(2,1)} %down_hbm.1, bf16[1,8192]{1,0:T(2,128)(2,1)} %residual_hbm.1, bf16[64,128]{1,0:T(8,128)(2,1)} %bitcast.5, bf16[504,4096]{1,0:T(8,128)(2,1)} %bitcast.4), custom_call_target="tpu_custom_call" | custom-call | tf_op jit(solution)/shard_map/scored_head/pallas_call | solution.py:561
  32.7 1.2 %slice_bitcast_fusion = f32[8]{0:T(128)} fusion(f32[1,128]{1,0:T(1,128)} %scored_head.1), kind=kLoop, calls=%fused_computation | loop fusion | bytes 64 | tf_op jit(solution)/shard_map/squeeze | solution.py:615

commit v6 on v4

--- a/solution.py
+++ b/solution.py
@@ -196,15 +196,25 @@
     for load in loads[:3]:
         load.start()
 
-    def down_copy(k):
-        return pltpu.make_async_copy(
-            down_hbm.at[:, pl.ds(pl.multiple_of(k * chunk_cols, chunk_cols), chunk_cols)],
-            down.at[k],
-            down_sem.at[k],
-        )
+    pieces = down_sem.shape[1]
+    piece_rows = block_cols // pieces
+
+    def down_copies(k):
+        return [
+            pltpu.make_async_copy(
+                down_hbm.at[
+                    p * piece_rows : (p + 1) * piece_rows,
+                    k * chunk_cols : (k + 1) * chunk_cols,
+                ],
+                down.at[k, p * piece_rows : (p + 1) * piece_rows],
+                down_sem.at[k, p],
+            )
+            for p in range(pieces)
+        ]
 
     for k in range(chunks):
-        down_copy(k).start()
+        for copy in down_copies(k):
+            copy.start()
     loads[4].start()
     loads[3].start()
 
@@ -268,7 +278,8 @@
     def await_chunk(a):
         for i in range(1, V):
             gated_arrival(a, i).wait_recv()
-        down_copy(a).wait()
+        for copy in down_copies(a):
+            copy.wait()
 
     def token_chunk(a):
         for s in range(V):
@@ -277,31 +288,30 @@
             )
         return gated_rows[a % 2].astype(jnp.bfloat16)
 
-    def term(gated, a, which):
+    def contract(left, right):
+        return lax.dot_general(
+            left, right, (((1,), (1,)), ((), ())), preferred_element_type=jnp.float32
+        )
+
+    def block(a, which, part):
         rows = pl.ds(pl.multiple_of(which * part_cols, part_cols), part_cols)
-        return lax.dot_general(
-            gated,
-            down[a, rows, :],
-            (((1,), (1,)), ((), ())),
-            preferred_element_type=jnp.float32,
-        )
+        return down[a, rows, part]
 
     theirs = jnp.zeros((T, part_cols), jnp.float32)
-    own = theirs
-    await_chunk(0)
-    gated = token_chunk(0)
+    own = jnp.zeros((part_cols, T), jnp.float32)
+    parts = [slice(k, k + MATRIX_SIDE) for k in range(0, chunk_cols, MATRIX_SIDE)]
     for a in range(chunks):
-        theirs = theirs + term(gated, a, other)
-        if a == chunks - 1:
-            update_out[...] = theirs
+        await_chunk(a)
+        gated = token_chunk(a)
+        if a < chunks - 1:
+            for part in parts:
+                theirs = theirs + contract(gated[:, part], block(a, other, part))
+                own = own + contract(block(a, m, part), gated[:, part])
+        else:
+            update_out[...] = theirs + contract(gated, block(a, other, slice(0, chunk_cols)))
             swap = remote(update_out, update_in, update_sem.at[0], update_sem.at[1], v, other)
             swap.start()
-            own = own + term(gated, a, m)
-        else:
-            await_chunk(a + 1)
-            following = token_chunk(a + 1)
-            own = own + term(gated, a, m)
-            gated = following
+            own = own + contract(block(a, m, slice(0, chunk_cols)), gated)
 
     loads[3].wait()
     loads[4].wait()
@@ -317,7 +327,7 @@
     for n in range(N):
         residual_rows[n : n + 1, :] = residual_in[n]
     swap.wait_recv()
-    stream = (residual_rows[...] + (own + update_in[...])).astype(jnp.bfloat16)
+    stream = (residual_rows[...] + (own.T + update_in[...])).astype(jnp.bfloat16)
     stream_out[...] = stream
     wide = stream.astype(jnp.float32)
     square_in[me] = to_lanes(jnp.sum(wide * wide, axis=1, keepdims=True))
@@ -499,6 +509,7 @@
         and T % 16 == 0
         and residual.shape[0] == 1
         and block_cols % (M * LANES) == 0
+        and block_cols % 64 == 0
         and width % (GATHER_CHUNKS * MATRIX_SIDE) == 0
         and half_width % (16 * LANES) == 0
     )
@@ -540,7 +551,7 @@
             pltpu.VMEM((T // M, vocab_cols), f32),
             pltpu.VMEM((V, 1, 3 * LANES), f32),
             dma((5,)),
-            dma((GATHER_CHUNKS,)),
+            dma((GATHER_CHUNKS, 4)),
             dma((GATHER_CHUNKS, V)),
             dma((GATHER_CHUNKS, V)),
             dma((N,)),

time: 30.9 us -> 33 us (1.068)
  Pallas kernels: 29.5 us -> 31.7 us
    pallas_call x1, Pallas kernels: 29.5 us -> 31.7 us  [body(): pl.pallas_call(functools.partial(kernel, V, M), out_shape=jax.ShapeDtypeS...]
where the time goes in v6:
time: 33 us; the launch traced here: 32.9 us
  Pallas kernels  31.7 us (96%)
  local copies, waits for them, and re-layouts  1.19 us (4%)
    pallas_call x1, Pallas kernels, body(): pl.pallas_call(functools.partial(kernel, V, M), out_shape=jax.ShapeDtypeS...  31.7 us
    squeeze x1, local copies, waits for them, and re-layouts, body(): return result[0, :targets.shape[0]]  1.19 us

profile of v6, /device:TPU:0, one launch (start us, length us, event | category | flops | bytes accessed | tf_op | source)
XLA Modules:
  0.0 32.9 jit_solution(12312708494787174237)
XLA Ops:
  0.0 31.7 %scored_head.1 = f32[1,128]{1,0:T(1,128)} custom-call(s32[8]{0:T(128)} %targets_ref.1, bf16[2,7168]{1,0:T(2,128)(2,1)} %gate_hbm.1, bf16[2,7168]{1,0:T(2,128)(2,1)} %up_hbm.1, bf16[1024,7168]{1,0:T(8,128)(2,1)} %down_hbm.1, bf16[1,8192]{1,0:T(2,128)(2,1)} %residual_hbm.1, bf16[64,128]{1,0:T(8,128)(2,1)} %bitcast.5, bf16[504,4096]{1,0:T(8,128)(2,1)} %bitcast.4), custom_call_target="tpu_custom_call" | custom-call | tf_op jit(solution)/shard_map/scored_head/pallas_call | solution.py:527
  31.7 1.2 %slice_bitcast_fusion = f32[8]{0:T(128)} fusion(f32[1,128]{1,0:T(1,128)} %scored_head.1), kind=kLoop, calls=%fused_computation | loop fusion | bytes 64 | tf_op jit(solution)/shard_map/squeeze | solution.py:581

commit v7 on v4

--- a/solution.py
+++ b/solution.py
@@ -133,6 +133,7 @@
     stats_in,
     in_sem,
     down_sem,
+    head_sem,
     gated_send,
     gated_recv,
     residual_send,
@@ -153,11 +154,11 @@
     N = V * M
     token_rows, width = gate.shape
     T = V * token_rows
-    block_cols = down.shape[1]
+    chunks, tiles, block_cols, _ = down.shape
     part_cols = block_cols // M
-    chunks, _, chunk_cols = down.shape
+    chunk_cols = tiles * LANES
     own_tokens = T // M
-    vocab_cols = head.shape[0]
+    vocab_cols = head.shape[1]
     half_owner = v // (V // M)
 
     def peer(i):
@@ -191,21 +192,30 @@
             gain,
             in_sem.at[3],
         ),
-        pltpu.make_async_copy(head_hbm, head, in_sem.at[4]),
     ]
     for load in loads[:3]:
         load.start()
 
-    def down_copy(k):
+    def down_copy(k, t):
+        first = pl.multiple_of((k * tiles + t) * LANES, LANES)
         return pltpu.make_async_copy(
-            down_hbm.at[:, pl.ds(pl.multiple_of(k * chunk_cols, chunk_cols), chunk_cols)],
-            down.at[k],
-            down_sem.at[k],
-        )
-
-    for k in range(chunks):
-        down_copy(k).start()
-    loads[4].start()
+            down_hbm.at[:, pl.ds(first, LANES)], down.at[k, t], down_sem.at[k, t]
+        )
+
+    def head_copy(t):
+        first = pl.multiple_of(t * LANES, LANES)
+        return pltpu.make_async_copy(
+            head_hbm.at[:, pl.ds(first, LANES)], head.at[t], head_sem.at[t]
+        )
+
+    def start_weights(k):
+        @pl.loop(0, tiles)
+        def _(t):
+            down_copy(k, t).start()
+
+    early = min(2, chunks)
+    for k in range(early):
+        start_weights(k)
     loads[3].start()
 
     def gated_copy(a, i):
@@ -258,6 +268,13 @@
             pl.semaphore_wait(barrier, N - 1)
         for i in range(1, V):
             gated_copy(a, i).start()
+    for k in range(early, chunks):
+        start_weights(k)
+
+    @pl.loop(0, head.shape[0])
+    def _(t):
+        head_copy(t).start()
+
     loads[2].wait()
     for n in range(N):
         residual_out[n] = own_residual[:, n * part_cols : (n + 1) * part_cols].astype(jnp.float32)
@@ -268,7 +285,10 @@
     def await_chunk(a):
         for i in range(1, V):
             gated_arrival(a, i).wait_recv()
-        down_copy(a).wait()
+
+        @pl.loop(0, tiles)
+        def _(t):
+            down_copy(a, t).wait()
 
     def token_chunk(a):
         for s in range(V):
@@ -281,7 +301,7 @@
         rows = pl.ds(pl.multiple_of(which * part_cols, part_cols), part_cols)
         return lax.dot_general(
             gated,
-            down[a, rows, :],
+            jnp.concatenate([down[a, t, rows, :] for t in range(tiles)], axis=1),
             (((1,), (1,)), ((), ())),
             preferred_element_type=jnp.float32,
         )
@@ -304,7 +324,11 @@
             gated = following
 
     loads[3].wait()
-    loads[4].wait()
+
+    @pl.loop(0, head.shape[0])
+    def _(t):
+        head_copy(t).wait()
+
     group = part_cols // LANES
     gains = gain[...].astype(jnp.float32)
     for j in range(V):
@@ -407,10 +431,9 @@
             normed = (stream_in[j].astype(jnp.float32) * scale * gain_rows[j]).astype(
                 jnp.bfloat16
             )
-            features = pl.ds(pl.multiple_of(j * part_cols, part_cols), part_cols)
             partial = partial + lax.dot_general(
                 normed,
-                head[:, features],
+                jnp.concatenate([head[j * group + q] for q in range(group)], axis=1),
                 (((1,), (1,)), ((), ())),
                 preferred_element_type=jnp.float32,
             )
@@ -521,11 +544,11 @@
         scratch_shapes=[
             pltpu.VMEM((token_rows, width), bf16),
             pltpu.VMEM((token_rows, width), bf16),
-            pltpu.VMEM((GATHER_CHUNKS, block_cols, chunk_cols), bf16),
+            pltpu.VMEM((GATHER_CHUNKS, chunk_cols // LANES, block_cols, LANES), bf16),
             pltpu.VMEM(residual.shape, bf16),
             pltpu.VMEM((half_width // LANES, LANES), bf16),
             pltpu.VMEM((slots, 1, part_cols), f32),
-            pltpu.VMEM((vocab_cols, half_width), bf16),
+            pltpu.VMEM((half_width // LANES, vocab_cols, LANES), bf16),
             pltpu.VMEM((GATHER_CHUNKS, V, token_rows, chunk_cols), bf16),
             pltpu.VMEM((2, T, chunk_cols), f32),
             pltpu.VMEM((N, 1, part_cols), f32),
@@ -539,8 +562,9 @@
             pltpu.VMEM((M, T // M, vocab_cols), f32),
             pltpu.VMEM((T // M, vocab_cols), f32),
             pltpu.VMEM((V, 1, 3 * LANES), f32),
-            dma((5,)),
-            dma((GATHER_CHUNKS,)),
+            dma((4,)),
+            dma((GATHER_CHUNKS, chunk_cols // LANES)),
+            dma((half_width // LANES,)),
             dma((GATHER_CHUNKS, V)),
             dma((GATHER_CHUNKS, V)),
             dma((N,)),

time: 30.9 us -> 31.9 us (1.032)
  Pallas kernels: 29.5 us -> 30.5 us
    pallas_call x1, Pallas kernels: 29.5 us -> 30.5 us  [body(): pl.pallas_call(functools.partial(kernel, V, M), out_shape=jax.ShapeDtypeS...]
where the time goes in v7:
time: 31.9 us; the launch traced here: 31.7 us
  Pallas kernels  30.5 us (96%)
  local copies, waits for them, and re-layouts  1.19 us (4%)
    pallas_call x1, Pallas kernels, body(): pl.pallas_call(functools.partial(kernel, V, M), out_shape=jax.ShapeDtypeS...  30.5 us
    squeeze x1, local copies, waits for them, and re-layouts, body(): return result[0, :targets.shape[0]]  1.19 us

profile of v7, /device:TPU:0, one launch (start us, length us, event | category | flops | bytes accessed | tf_op | source)
XLA Modules:
  0.0 31.7 jit_solution(8249461107242122361)
XLA Ops:
  0.0 30.5 %scored_head.1 = f32[1,128]{1,0:T(1,128)} custom-call(s32[8]{0:T(128)} %targets_ref.1, bf16[2,7168]{1,0:T(2,128)(2,1)} %gate_hbm.1, bf16[2,7168]{1,0:T(2,128)(2,1)} %up_hbm.1, bf16[1024,7168]{1,0:T(8,128)(2,1)} %down_hbm.1, bf16[1,8192]{1,0:T(2,128)(2,1)} %residual_hbm.1, bf16[64,128]{1,0:T(8,128)(2,1)} %bitcast.5, bf16[504,4096]{1,0:T(8,128)(2,1)} %bitcast.4), custom_call_target="tpu_custom_call" | custom-call | tf_op jit(solution)/shard_map/scored_head/pallas_call | solution.py:539
  30.5 1.2 %slice_bitcast_fusion = f32[8]{0:T(128)} fusion(f32[1,128]{1,0:T(1,128)} %scored_head.1), kind=kLoop, calls=%fused_computation | loop fusion | bytes 64 | tf_op jit(solution)/shard_map/squeeze | solution.py:594

commit v8 on v4

--- a/solution.py
+++ b/solution.py
@@ -78,7 +78,7 @@
     return merged[2] - merged[0] - jnp.log(merged[1])
 
 
-GATHER_CHUNKS = 4
+GATHER_CHUNKS = 7
 MATRIX_SIDE = 256
 LANES = 128
 
@@ -290,18 +290,20 @@
     own = theirs
     await_chunk(0)
     gated = token_chunk(0)
-    for a in range(chunks):
+    for a in range(chunks - 2):
         theirs = theirs + term(gated, a, other)
-        if a == chunks - 1:
-            update_out[...] = theirs
-            swap = remote(update_out, update_in, update_sem.at[0], update_sem.at[1], v, other)
-            swap.start()
-            own = own + term(gated, a, m)
-        else:
-            await_chunk(a + 1)
-            following = token_chunk(a + 1)
-            own = own + term(gated, a, m)
-            gated = following
+        await_chunk(a + 1)
+        following = token_chunk(a + 1)
+        own = own + term(gated, a, m)
+        gated = following
+    last = chunks - 1
+    theirs = theirs + term(gated, last - 1, other)
+    await_chunk(last)
+    following = token_chunk(last)
+    update_out[...] = theirs + term(following, last, other)
+    swap = remote(update_out, update_in, update_sem.at[0], update_sem.at[1], v, other)
+    swap.start()
+    own = own + term(gated, last - 1, m) + term(following, last, m)
 
     loads[3].wait()
     loads[4].wait()

time: 30.9 us -> 30.8 us (level)
  no operation moved by 1% of the time
where the time goes in v8:
time: 30.8 us; the launch traced here: 30.7 us
  Pallas kernels  29.5 us (96%)
  local copies, waits for them, and re-layouts  1.19 us (4%)
    pallas_call x1, Pallas kernels, body(): pl.pallas_call(functools.partial(kernel, V, M), out_shape=jax.ShapeDtypeS...  29.5 us
    squeeze x1, local copies, waits for them, and re-layouts, body(): return result[0, :targets.shape[0]]  1.19 us

profile of v8, /device:TPU:0, one launch (start us, length us, event | category | flops | bytes accessed | tf_op | source)
XLA Modules:
  0.0 30.7 jit_solution(575112947409142914)
XLA Ops:
  0.0 29.5 %scored_head.1 = f32[1,128]{1,0:T(1,128)} custom-call(s32[8]{0:T(128)} %targets_ref.1, bf16[2,7168]{1,0:T(2,128)(2,1)} %gate_hbm.1, bf16[2,7168]{1,0:T(2,128)(2,1)} %up_hbm.1, bf16[1024,7168]{1,0:T(8,128)(2,1)} %down_hbm.1, bf16[1,8192]{1,0:T(2,128)(2,1)} %residual_hbm.1, bf16[64,128]{1,0:T(8,128)(2,1)} %bitcast.5, bf16[504,4096]{1,0:T(8,128)(2,1)} %bitcast.4), custom_call_target="tpu_custom_call" | custom-call | tf_op jit(solution)/shard_map/scored_head/pallas_call | solution.py:518
  29.5 1.2 %slice_bitcast_fusion = f32[8]{0:T(128)} fusion(f32[1,128]{1,0:T(1,128)} %scored_head.1), kind=kLoop, calls=%fused_computation | loop fusion | bytes 64 | tf_op jit(solution)/shard_map/squeeze | solution.py:572

commit v9 on v8

--- a/solution.py
+++ b/solution.py
@@ -176,12 +176,6 @@
             device_id_type=pl.DeviceIdType.MESH,
         )
 
-    barrier = pltpu.get_barrier_semaphore()
-    for i in range(1, N):
-        pl.semaphore_signal(
-            barrier, inc=1, device_id=coords(peer(i)), device_id_type=pl.DeviceIdType.MESH
-        )
-
     loads = [
         pltpu.make_async_copy(gate_hbm, gate, in_sem.at[0]),
         pltpu.make_async_copy(up_hbm, up, in_sem.at[1]),
@@ -195,6 +189,12 @@
     ]
     for load in loads[:3]:
         load.start()
+
+    barrier = pltpu.get_barrier_semaphore()
+    for i in range(1, N):
+        pl.semaphore_signal(
+            barrier, inc=1, device_id=coords(peer(i)), device_id_type=pl.DeviceIdType.MESH
+        )
 
     def down_copy(k):
         return pltpu.make_async_copy(

time: 30.8 us -> 30.1 us (0.977)
  Pallas kernels: 29.5 us -> 28.8 us
    pallas_call x1, Pallas kernels: 29.5 us -> 28.8 us  [body(): pl.pallas_call(functools.partial(kernel, V, M), out_shape=jax.ShapeDtypeS...]
where the time goes in v9:
time: 30.1 us; the launch traced here: 30 us
  Pallas kernels  28.8 us (96%)
  local copies, waits for them, and re-layouts  1.19 us (4%)
    pallas_call x1, Pallas kernels, body(): pl.pallas_call(functools.partial(kernel, V, M), out_shape=jax.ShapeDtypeS...  28.8 us
    squeeze x1, local copies, waits for them, and re-layouts, body(): return result[0, :targets.shape[0]]  1.19 us

profile of v9, /device:TPU:0, one launch (start us, length us, event | category | flops | bytes accessed | tf_op | source)
XLA Modules:
  0.0 30.0 jit_solution(4050956568553608491)
XLA Ops:
  0.0 28.8 %scored_head.1 = f32[1,128]{1,0:T(1,128)} custom-call(s32[8]{0:T(128)} %targets_ref.1, bf16[2,7168]{1,0:T(2,128)(2,1)} %gate_hbm.1, bf16[2,7168]{1,0:T(2,128)(2,1)} %up_hbm.1, bf16[1024,7168]{1,0:T(8,128)(2,1)} %down_hbm.1, bf16[1,8192]{1,0:T(2,128)(2,1)} %residual_hbm.1, bf16[64,128]{1,0:T(8,128)(2,1)} %bitcast.5, bf16[504,4096]{1,0:T(8,128)(2,1)} %bitcast.4), custom_call_target="tpu_custom_call" | custom-call | tf_op jit(solution)/shard_map/scored_head/pallas_call | solution.py:518
  28.8 1.2 %slice_bitcast_fusion = f32[8]{0:T(128)} fusion(f32[1,128]{1,0:T(1,128)} %scored_head.1), kind=kLoop, calls=%fused_computation | loop fusion | bytes 64 | tf_op jit(solution)/shard_map/squeeze | solution.py:572
